TPU v7x, 32 devices: a whole 2x2x4 slice. The times are simulated.
32 devices in a mesh: dp: 8 (over z, x), tm: 4 (over y, core).
Axes of the slice: x: 2, y: 2, z: 4, core: 2. Of those that a mesh axis runs over, the one named last changes fastest.
Arguments:
- inputs: bfloat16 [32, 2048, 512], P('dp', 'tm'), may hold values from -6 to 6
- lengths: int32 [32], replicated, may hold values from 128 to 2048, as said below
- depth_w: bfloat16 [5, 5, 512], P(None, None, ('dp', 'tm')), may hold values from -2.5 to 2.5
- point_w: bfloat16 [5, 512, 512], P(None, ('dp', 'tm')), may hold values from -0.25 to 0.25
- gamma: bfloat16 [5, 512], P(None, ('dp', 'tm')), may hold values from 0.5 to 1.5
- beta: bfloat16 [5, 512], P(None, ('dp', 'tm')), may hold values from -3 to 3
- squeeze_w: bfloat16 [512, 64], P(('dp', 'tm')), may hold values from -0.5 to 0.5
- excite_w: bfloat16 [64, 512], P(None, ('dp', 'tm')), may hold values from -1.5 to 1.5
- resid_w: bfloat16 [512, 512], P(('dp', 'tm')), may hold values from -0.25 to 0.25
- cotangent: bfloat16 [32, 2048, 512], P('dp', 'tm'), may hold values from -6 to 6
Outputs:
- output: bfloat16 [32, 2048, 512], P('dp', 'tm')
- grad_inputs: bfloat16 [32, 2048, 512], P('dp', 'tm')
- grad_depth: float32 [5, 5, 512], P(None, None, ('dp', 'tm'))
- grad_point: float32 [5, 512, 512], P(None, ('dp', 'tm'))
- grad_gamma: float32 [5, 512], P(None, ('dp', 'tm'))
- grad_beta: float32 [5, 512], P(None, ('dp', 'tm'))
- grad_squeeze: float32 [512, 64], P(('dp', 'tm'))
- grad_excite: float32 [64, 512], P(None, ('dp', 'tm'))
- grad_resid: float32 [512, 512], P(('dp', 'tm'))
Inputs may be any that keep to these rules, and one draw needn't show every extreme that they name: `lengths`: each aligned block of 4 utterances holds exactly one of length 2048; the others have at most 512 frames.
All inputs are finite; a program needn't handle non-finite values.
Results may differ from a plain program's by a relative error of at most 0.025.
Values may be sent and summed in bfloat16 or wider, within the bound.
A program may use at most 128 MiB of HBM per device.

v0:
```python
import functools

import jax
import jax.numpy as jnp
from jax import lax
from jax.experimental import pallas as pl
from jax.experimental.pallas import tpu as pltpu
from jax.sharding import PartitionSpec as P

MESH = pl.DeviceIdType.MESH
NORM_EPSILON = 1e-05
LANES = 128
HIGHEST = lax.Precision.HIGHEST
F32 = jnp.float32
BF16 = jnp.bfloat16


def dot(a, b, dims=((1,), (0,)), precision=None):
    return lax.dot_general(a, b, (dims, ((), ())), precision=precision, preferred_element_type=F32)


def logistic(v):
    return 0.5 * jnp.tanh(0.5 * v) + 0.5


def dot_parts(v, w, dims=((1,), (0,))):
    rows, parts = v.shape[0], []
    for _ in range(3):
        part = v.astype(BF16)
        parts.append(part.astype(F32))
        v = v - parts[-1]
    total = dot(jnp.concatenate(parts, axis=0).astype(BF16), w, dims)
    return total[0:rows] + total[rows : 2 * rows] + total[2 * rows :]


def block_kernel(cfg, names, *refs):
    DP, TM, U, F, C, SE, SH, LAYERS, KERNEL, fast = cfg
    env = dict(zip(names, refs, strict=True))
    lengths, x_any, g_any = env["lengths"], env["x_any"], env["g_any"]
    out_any, gin_any = env["out_any"], env["gin_any"]
    xv, xs, edge, xin, gin4 = env["xv"], env["xs"], env["edge"], env["xin"], env["gin4"]
    halo_l, halo_r, cot, ypad, dlow = env["halo_l"], env["halo_r"], env["cot"], env["ypad"], env["dlow"]
    pre, hh, mask, hmask, coef = env["pre"], env["hh"], env["mask"], env["hmask"], env["coef"]
    resd, act, du, drl = env["resd"], env["act"], env["du"], env["drl"]
    dn, gres_in = act, resd
    dhl, ddpad = env["dhl"], env["ddpad"]
    perm_l, perm_s, back_l, back_s = env["perm_l"], env["perm_s"], env["back_l"], env["back_s"]
    outp, obuf, gbuf, gp, small = env["outp"], env["obuf"], env["gbuf"], env.get("gp"), env["small"]
    sums, send_a, send_b, recv_core, recv_chip = (
        env["sums"], env["send_a"], env["send_b"], env["recv_core"], env["recv_chip"]
    )
    hsend, dhh, tsend, trecv = env["hsend"], env["dhh"], env["tsend"], env["trecv"]
    pool, gate, cvec, gsmall = env["pool"], env["gate"], env["cvec"], env["gsmall"]
    hx = env["hx"]
    slope, fac, facs = env["slope"], env["fac"], env["facs"]
    ggb = env["ggb"]
    sem_loc, sem_cs, sem_cr, sem_ks, sem_kr = (
        env["sem_loc"], env["sem_cs"], env["sem_cr"], env["sem_ks"], env["sem_kr"]
    )
    sem_cot = env["sem_cot"]
    sem_hs, sem_hr, sem_ts, sem_tr = env["sem_hs"], env["sem_hr"], env["sem_ts"], env["sem_tr"]
    sem_xs, sem_xr, sem_os, sem_or = env["sem_xs"], env["sem_xr"], env["sem_os"], env["sem_or"]
    MATS = LAYERS + 1
    AT_TAPS, AT_GAMMA = SE, SE + 8 * LAYERS
    AT_BETA = AT_GAMMA + 8
    NL = C // LANES
    UR = F // 4
    NU = 4 + (U - 1)
    NB = UR // 16
    R = NU * UR
    N_SRC = TM // 4
    dp, tm = lax.axis_index("dp"), lax.axis_index("tm")
    partner = tm + 1 - 2 * lax.rem(tm, 2)
    first, last = tm == 0, tm == TM - 1
    chips = [(a, 2 * b) for a in range(DP) for b in range(TM // 2) if a or b]
    n_chips = len(chips) + 1
    my_chip = dp * (TM // 2) + tm // 2

    def turns(v, n):
        bits = [1 << i for i in range(n.bit_length() - 1)] if n & (n - 1) == 0 else []
        return [(bit, bit * (1 - 2 * lax.rem(v // bit, 2))) for bit in bits]

    flips = {}

    def other(name, v, a, n):
        if name not in flips:
            flips[name] = turns(v, n)
        if not flips[name]:
            return lax.rem(v + a, n) if n > 1 else v
        for bit, step in flips[name]:
            if a & bit:
                v = v + step
        return v

    def at_chip(offset):
        return (lax.rem(dp + offset[0], DP), lax.rem(tm + offset[1], TM))

    def win(u):
        return u * UR if u < 4 else F + 64 + (u - 4) * (UR + 64)

    def seg_of(u):
        return 0 if u < 4 else u - 3

    def lane(j):
        return slice(j * LANES, (j + 1) * LANES)

    def each_lane(body):
        for j in range(NL):
            body(j, 0)

    def wide(v):
        return jnp.concatenate([v] * NL, axis=1)

    def remote(src, dst, ssem, rsem, dev):
        return pltpu.make_async_remote_copy(src, dst, ssem, rsem, device_id=dev, device_id_type=MESH)

    def total_wait(ref, sem):
        pltpu.make_async_copy(ref, ref, sem).wait()

    barrier = pltpu.get_barrier_semaphore()
    load_x = pltpu.make_async_copy(x_any, xv, sem_loc.at[0])
    load_x.start()
    others = [(0, b) for b in range(1, TM, 2)]
    for offset in chips + others:
        pl.semaphore_signal(barrier, inc=1, device_id=at_chip(offset), device_id_type=MESH)

    x, z, y, core = lax.rem(dp, 2), dp // 2, tm // 2, lax.rem(tm, 2)
    Y = TM // 2
    Z = DP // 2

    my_len = [lengths[dp * U + b] for b in range(U)]
    long_at = jnp.int32(0)
    for b in range(1, U):
        long_at = jnp.where(my_len[b] == F * TM, jnp.int32(b), long_at)
    short_at = [jnp.where(k < long_at, k, k + 1) for k in range(U - 1)]
    short_len = [lengths[dp * U + b] for b in range(U - 1)]
    short_len = [jnp.where(k < long_at, my_len[k], my_len[k + 1]) for k in range(U - 1)]
    count = lax.fori_loop(0, DP * U, lambda i, c: c + lengths[i], jnp.int32(0)).astype(F32)
    inv_count = 1.0 / jnp.full((1, LANES), count, F32)
    def make_masks():
        rows = lax.broadcasted_iota(jnp.int32, (UR, LANES), 0)
        time_s = (rows & 15) * NB + (rows >> 4) + tm * UR
        for k in range(U - 1):
            mask[k * UR : (k + 1) * UR, :] = jnp.where(time_s < short_len[k], 1.0, 0.0)
        e16 = lax.broadcasted_iota(jnp.int32, (16, LANES), 0)
        part = (e16 & 7) >> 1
        is_left = e16 < 8
        when = jnp.where(is_left, tm * UR - 2 + (e16 & 1), tm * UR + UR + (e16 & 1))
        bound = jnp.full((16, LANES), 1 << 30, jnp.int32)
        for k in range(U - 1):
            bound = jnp.where(part == k + 1, short_len[k], bound)
        inside = jnp.where(is_left, tm, TM - 1 - tm) > 0
        hmask[...] = jnp.where(inside & (when < bound), 1.0, 0.0)

    def one_hot(ref, size, to_time):
        n = size // 16
        r0 = lax.broadcasted_iota(jnp.int32, (UR, size), 0)
        r1 = lax.broadcasted_iota(jnp.int32, (UR, size), 1)
        for c in range(size // UR):
            a, b = (r1, r0 + c * UR) if to_time else (r0 + c * UR, r1)
            hit = b == (a & 15) * n + (a >> 4)
            ref[c * UR : (c + 1) * UR, :] = jnp.where(hit, 1.0, 0.0).astype(BF16)

    def zero_ends():
        @pl.when(first)
        def _():
            halo_l[...] = jnp.zeros(halo_l.shape, BF16)
            for l in range(LAYERS):
                hh[l, 0:8, :] = jnp.zeros((8, C), F32)
                dhh[l, 0:8, :] = jnp.zeros((8, C), F32)

        @pl.when(last)
        def _():
            halo_r[...] = jnp.zeros(halo_r.shape, BF16)
            for l in range(LAYERS):
                hh[l, 8:16, :] = jnp.zeros((8, C), F32)
                dhh[l, 8:16, :] = jnp.zeros((8, C), F32)

    def stage_short():
        @pl.when(tm < N_SRC)
        def _():
            for k in range(U - 1):
                def cp(c, _):
                    sl = pl.ds(pl.multiple_of(c * UR, UR), UR)
                    xs[k, sl, :] = xv[short_at[k], sl, :]
                    return 0
                lax.fori_loop(0, 4, cp, 0)

    def send_short(dst, half):
        def act_on(d):
            if half == 0:
                d.start()
            else:
                d.wait_send()

        @pl.when(tm < N_SRC)
        def _():
            for q in range(4):
                chunk = 4 * tm + q
                main = xs.at[:, q * UR : (q + 1) * UR, :]
                head = xs.at[:, q * UR : q * UR + 16, :]
                tail = xs.at[:, (q + 1) * UR - 16 : (q + 1) * UR, :]

                def go_main():
                    act_on(remote(main, dst, sem_xs.at[q], sem_xr.at[0], (dp, chunk)))

                def go_head():
                    act_on(remote(head, halo_r.at[1:U], sem_xs.at[4 + q], sem_xr.at[1], (dp, chunk - 1)))

                if q == 0:
                    pl.when(tm > 0)(go_main)
                    if half == 0:
                        @pl.when(tm == 0)
                        def _():
                            for k in range(U - 1):
                                dst[k] = xs[k, 0:UR, :]
                else:
                    go_main()
                if q < 2:
                    pl.when(tm > 0)(go_head)
                else:
                    go_head()
                if q == 1 and half == 0:
                    @pl.when(tm == 0)
                    def _():
                        for k in range(U - 1):
                            halo_r[1 + k] = xs[k, UR : UR + 16, :]

                @pl.when(chunk + 1 < TM)
                def _():
                    act_on(remote(tail, halo_l.at[1:U], sem_xs.at[8 + q], sem_xr.at[2], (dp, chunk + 1)))

    S2 = 2 * LAYERS

    def cot_piece(k, half):
        @pl.when(tm < N_SRC)
        def _():
            for q in range(4):
                chunk = 4 * tm + q
                src = xs.at[k, q * UR : (q + 1) * UR, :]
                copy = remote(src, gin4.at[k], sem_cot.at[k, q], sem_cr.at[S2 + k], (dp, chunk))
                go = copy.start if half == 0 else copy.wait_send
                if q == 0:
                    pl.when(tm > 0)(go)
                else:
                    go()

        if half == 0:
            @pl.when(tm == 0)
            def _():
                gin4[k] = xs[k, 0:UR, :]

    def recv_short(dst):
        @pl.when(tm > 0)
        def _():
            total_wait(dst, sem_xr.at[0])
            total_wait(halo_l.at[1:U], sem_xr.at[2])

            @pl.when(tm < TM - 1)
            def _():
                total_wait(halo_r.at[1:U], sem_xr.at[1])

    def edges(send, recv_l, recv_r, ssem, rsem, start):
        to_next = remote(send.at[1], recv_l, ssem.at[0], rsem.at[0], (dp, lax.rem(tm + 1, TM)))
        to_prev = remote(send.at[0], recv_r, ssem.at[1], rsem.at[1], (dp, lax.rem(tm + TM - 1, TM)))
        if start:
            pl.when(tm < TM - 1)(lambda: to_next.start())
            pl.when(tm > 0)(lambda: to_prev.start())
        else:
            @pl.when(tm < TM - 1)
            def _():
                to_next.wait_send()
                to_prev.wait_recv()

            @pl.when(tm > 0)
            def _():
                to_prev.wait_send()
                to_next.wait_recv()

    for name, v, n in (("dp", dp, DP), ("y", y, Y), ("z", z, Z)):
        other(name, v, 0, n)

    def plane_peers():
        return [(a, b) for a in reversed(range(Z)) for b in reversed(range(Y)) if a or b]

    def plane_peer(offset):
        pz, py = other("z", z, offset[0], Z), other("y", y, offset[1], Y)
        return pz, py, (2 * pz + x, 2 * py + core)

    across = (2 * z + 1 - x, tm)

    def gather_stage(buf, m, stage):
        ss, rs = env["sem_gs"].at[m, stage], env["sem_gr"].at[m, stage]
        if stage == 0:
            mine = buf.at[z, x, y, core]
            for offset in plane_peers():
                remote(mine, mine, ss, rs, plane_peer(offset)[2]).start()
        elif stage == 1:
            mine = buf.at[:, x, :, core]
            remote(mine, mine, ss, rs, across).start()
        else:
            mine = buf.at[:, :, :, core]
            remote(mine, mine, ss, rs, (dp, partner)).start()

    def gather_wait(buf, m, stage, sems):
        if stage == 0:
            size = env["little_rz"].at[0] if buf is sall else env["big_rz"].at[0]
            total_wait(size, sems.at[m, stage])
        elif stage == 1:
            total_wait(buf.at[:, 0, :, 0], sems.at[m, stage])
        else:
            total_wait(buf.at[:, :, :, 0], sems.at[m, stage])

    def gather_got(buf, m, stage):
        gather_wait(buf, m, stage, env["sem_gr"])

    def gather_left(buf, m):
        for stage in range(3):
            gather_wait(buf, m, stage, env["sem_gs"])

    if fast:
        wall, sall = env["wall"], env["sall"]
        halves = [(wall.at[0], 0)]

        def weights(m):
            return wall[m].reshape(C, C)

        pack = env["pack"]
        pack[...] = jnp.zeros(pack.shape, F32)
        for l in range(LAYERS):
            pack[AT_TAPS + 8 * l : AT_TAPS + 8 * l + KERNEL, 0:SH] = env["taps"][l].astype(F32)
        pack[AT_GAMMA : AT_GAMMA + LAYERS, 0:SH] = env["gamma"][...].astype(F32)
        pack[AT_BETA : AT_BETA + LAYERS, 0:SH] = env["beta"][...].astype(F32)
        turned = pack[...].T[0:SH]
        pack[0:SH, :] = turned
        pack[0:SH, 0:SE] = env["excite"][...].astype(F32)
        sall[z, x, y, core, :, 0:LANES] = pack[0:SH, :].astype(BF16)
        pack[0:SH, 0:SE] = env["squeeze"][...].astype(F32)
        sall[z, x, y, core, :, LANES : 2 * LANES] = pack[0:SH, :].astype(BF16)
        for l in range(LAYERS):
            wall[l, z, x, y, core] = env["point"][l]
        wall[LAYERS, z, x, y, core] = env["resid"][...]
    else:
        def weights(m):
            return env["mats"][m]

        small[...] = env["small_in"][...]

    def squeeze_all():
        if fast:
            return sall[...].reshape(C, 2 * LANES)[:, LANES : LANES + SE]
        return env["squeeze"][...]

    class Scatter:
        def __init__(self, name):
            self.send, self.core, self.xsum, self.rx, self.zsum, self.rz, self.ss, self.rs = (
                env[name + part] for part in ("_send", "_core", "_xsum", "_rx", "_zsum", "_rz", "_ss", "_rs")
            )
            self.dtype = self.send.dtype

        def go(self, m, stage):
            ss, rs = self.ss.at[m, stage], self.rs.at[m, stage]
            if stage == 0:
                remote(self.send.at[m, :, :, :, 1 - core], self.core.at[m], ss, rs, (dp, partner)).start()
            elif stage == 1:
                remote(self.xsum.at[m, 1 - x], self.rx.at[m], ss, rs, across).start()
            else:
                for i, offset in enumerate(plane_peers()):
                    pz, py, peer = plane_peer(offset)
                    remote(self.zsum.at[m, pz, py], self.rz.at[m, i], ss, rs, peer).start()

        def wait(self, m, stage, sems):
            total_wait((self.core.at[m], self.rx.at[m], self.rz.at[m])[stage], sems.at[m, stage])

        def left(self, m):
            for stage in range(3):
                self.wait(m, stage, self.ss)

        def core_to_x(self, m):
            self.wait(m, 0, self.rs)

            def body(i, _):
                v = self.send[m, i, :, :, core].astype(F32) + self.core[m, i].astype(F32)
                for k in range(2):
                    self.xsum[m, k, i] = v[k].astype(self.dtype)
                return 0

            lax.fori_loop(0, Z, body, 0)
            self.go(m, 1)

        def x_to_plane(self, m):
            self.x_sum(m)
            self.go(m, 2)

        def x_sum(self, m):
            self.wait(m, 1, self.rs)

            def body(i, _):
                v = self.xsum[m, x, i].astype(F32) + self.rx[m, i].astype(F32)
                self.zsum[m, i] = v.astype(self.dtype)
                return 0

            lax.fori_loop(0, Z, body, 0)

        def result(self, m):
            self.wait(m, 2, self.rs)
            v = self.zsum[m, z, y].astype(F32)
            for i in range(Z * Y - 1):
                v = v + self.rz[m, i].astype(F32)
            return v

    if fast:
        big, little = Scatter("big"), Scatter("little")

    def to_perm_long(src, dst, base):
        for u in range(4):
            o = base(u)
            dst[o : o + UR, :] = dot(perm_l[u * UR : (u + 1) * UR, :], src).astype(BF16)

    def to_perm_short(src, dst, base, masked):
        for k in range(U - 1):
            v = dot(perm_s[...], src[k])
            if masked:
                v = v * wide(mask[k * UR : (k + 1) * UR, :])
            o = base(4 + k)
            dst[o : o + UR, :] = v.astype(BF16)

    y0 = ypad.at[0]
    zero_ends()
    pl.semaphore_wait(barrier, len(chips) + len(others))
    if fast:
        gather_stage(sall, MATS, 0)
        for buf, m in halves:
            gather_stage(buf, m, 0)
    load_x.wait()
    edge[0] = xv[long_at, 0:16, :]
    edge[1] = xv[long_at, F - 16 : F, :]
    stage_short()
    edge_sems = (sem_xs.at[pl.ds(12, 2)], sem_xr.at[pl.ds(3, 2)])
    edges(edge, halo_l.at[0], halo_r.at[0], *edge_sems, True)
    send_short(xin, 0)
    if fast:
        for m in range(1, min(3, MATS)):
            gather_stage(wall.at[m], m, 0)
    one_hot(perm_l, F, False)
    one_hot(perm_s, UR, False)
    to_perm_long(xv[long_at], y0, lambda u: win(u) + 32)
    load_g = pltpu.make_async_copy(g_any, xv, sem_loc.at[0])
    load_g.start()
    make_masks()
    if fast:
        gather_got(sall, MATS, 0)
        gather_stage(sall, MATS, 1)
        for buf, m in halves:
            gather_got(buf, m, 0)
            gather_stage(buf, m, 1)
        gather_got(sall, MATS, 1)
        gather_stage(sall, MATS, 2)
        for buf, m in halves:
            gather_got(buf, m, 1)
            gather_stage(buf, m, 2)
        gather_got(sall, MATS, 2)
        for j in range(NL):
            part = sall[...].reshape(C, 2 * LANES)[j * LANES : (j + 1) * LANES, 0:LANES].astype(F32)
            small[:, j * LANES : (j + 1) * LANES] = part.T

    def fill_pads(ref, row0, n, j, b0, b1, b2, b3, halo, seg):
        e = lax.broadcasted_iota(jnp.int32, (16, LANES), 0)

        def put(at, v):
            ref[pl.ds(row0 + at * 16, 16), lane(j)] = v.astype(BF16)

        put(0, jnp.where(e == 0, halo[2 * seg : 2 * seg + 1], pltpu.roll(b2, 1, 0)))
        put(1, jnp.where(e == 0, halo[2 * seg + 1 : 2 * seg + 2], pltpu.roll(b3, 1, 0)))
        put(n + 2, jnp.where(e == 15, halo[8 + 2 * seg : 9 + 2 * seg], pltpu.roll(b0, 15, 0)))
        put(n + 3, jnp.where(e == 15, halo[9 + 2 * seg : 10 + 2 * seg], pltpu.roll(b1, 15, 0)))

    def pads_from(ref, j, halo, segs):
        for seg in segs:
            u0, u1 = (0, 3) if seg == 0 else (3 + seg, 3 + seg)
            n = F // 16 if seg == 0 else NB
            o0, o1 = win(u0) + 32, win(u1) + 32 + UR
            blk = [ref[o : o + 16, lane(j)].astype(F32) for o in (o0, o0 + 16, o1 - 32, o1 - 16)]
            fill_pads(ref, win(u0), n, j, *blk, halo, seg)

    def first_pads(segs):
        def body(j, _):
            none = jnp.zeros((2, LANES), F32)
            left = [halo_l[s, :, lane(j)].astype(F32)[14:16] if s in segs else none for s in range(4)]
            right = [halo_r[s, :, lane(j)].astype(F32)[0:2] if s in segs else none for s in range(4)]
            halo = jnp.where(hmask[...] > 0.0, jnp.concatenate(left + right, axis=0), 0.0)
            pads_from(y0, j, halo, segs)
            return 0

        each_lane(body)

    edges(edge, halo_l.at[0], halo_r.at[0], *edge_sems, False)
    first_pads([0])

    def shorts_arrive():
        if fast:
            gather_got(wall.at[1], 1, 0)
            gather_stage(wall.at[1], 1, 1)
        recv_short(xin)
        to_perm_short(xin, y0, lambda u: win(u) + 32, True)
        send_short(xin, 1)
        first_pads(range(1, U))

    def sync_core(s, meanwhile):
        d = remote(send_a.at[s], recv_core.at[s], sem_cs.at[s], sem_cr.at[s], (dp, partner))
        d.start()
        meanwhile()
        d.wait()
        send_b[s] = send_a[s] + recv_core[s]

    def sync_send(s):
        recv_chip[s, my_chip] = send_b[s]
        dst = recv_chip.at[s, my_chip]

        for a in reversed(range(DP)):
            for b in reversed(range(Y)):
                if a or b:
                    there = (other("dp", dp, a, DP), 2 * other("y", y, b, Y) + core)
                    remote(send_b.at[s], dst, sem_ks.at[s], sem_kr.at[s], there).start()

    def sync_done(s):
        others = recv_chip.at[s, 0 : n_chips - 1]
        total_wait(others, sem_kr.at[s])
        total_wait(others, sem_ks.at[s])
        terms = [recv_chip[s, i] for i in range(n_chips)]
        while len(terms) > 1:
            terms = [sum(terms[i : i + 2][1:], terms[i]) for i in range(0, len(terms), 2)]
        return terms[0]

    def tap_rows(l, j):
        group = small[pl.ds(pl.multiple_of(AT_TAPS + 8 * l, 8), 8), lane(j)]
        return [group[k : k + 1] for k in range(KERNEL)]

    LONG, SHORT = range(4), range(4, NU)

    def conv_pass(l, units):
        def body(j, _):
            w = tap_rows(l, j)
            for u in units:
                o = win(u)
                v = ypad[l, o : o + UR + 64, lane(j)].astype(F32)
                t = v[0:UR] * w[0]
                for k in range(1, KERNEL):
                    t = t + v[16 * k : 16 * k + UR] * w[k]
                if u >= 4:
                    t = t * mask[(u - 4) * UR : (u - 3) * UR, :]
                dlow[l, u * UR : (u + 1) * UR, lane(j)] = t.astype(BF16)
            return 0

        each_lane(body)

    def fold8(v):
        return jnp.sum(v.reshape(v.shape[0] // 8, 8, v.shape[1]), axis=0)

    def put_edges(src, l):
        for seg in range(4):
            base = 0 if seg == 0 else F + (seg - 1) * UR
            n = F if seg == 0 else UR
            for e in range(2):
                hsend[l, 1, 2 * seg + e : 2 * seg + e + 1, :] = src(base + n - 32 + 16 * e + 15)
                hsend[l, 0, 2 * seg + e : 2 * seg + e + 1, :] = src(base + 16 * e)

    def matmul_pass(l, units):
        r = slice(units[0] * UR, (units[-1] + 1) * UR)
        h = dot(dlow[l, r, :], weights(l))
        pre[l, r, :] = h
        s0, s1 = fold8(h), fold8(h * h)
        if units[0] > 0:
            s0, s1 = s0 + sums[0], s1 + sums[1]
        sums[0] = s0
        sums[1] = s1

    def send_stats(l):
        send_a[l, 0:1, :] = jnp.sum(sums[0], axis=0, keepdims=True)
        send_a[l, 1:2, :] = jnp.sum(sums[1], axis=0, keepdims=True)

    def act_pass(l):
        def body(j, _):
            a, b = coef[l, 0:1, lane(j)], coef[l, 1:2, lane(j)]
            for u in range(NU):
                v = pre[l, u * UR : (u + 1) * UR, lane(j)] * a + b
                v = v + v * jnp.tanh(v)
                if u >= 4:
                    v = v * mask[(u - 4) * UR : (u - 3) * UR, :]
                o = win(u) + 32
                ypad[l + 1, o : o + UR, lane(j)] = v.astype(BF16)
            v = hh[l, :, lane(j)] * a + b
            v = (v + v * jnp.tanh(v)) * hmask[...]
            pads_from(ypad.at[l + 1], j, v, range(U))
            return 0

        each_lane(body)

    def prep_pass(l):
        def body(j, _):
            a, b, m, i = (coef[l, r : r + 1, lane(j)] for r in range(4))
            for u in range(NU):
                rs = slice(u * UR, (u + 1) * UR)
                h = pre[l, rs, lane(j)]
                half = h * a + b
                t = jnp.tanh(half)
                v = (0.5 + 0.5 * t) * (1.0 + half * (1.0 - t))
                if u >= 4:
                    v = v * mask[(u - 4) * UR : (u - 3) * UR, :]
                slope[l, rs, lane(j)] = v.astype(BF16)
                pre[l, rs, lane(j)] = (h - m) * i
            hx[l, :, lane(j)] = (hh[l, :, lane(j)] - m) * i
            return 0

        each_lane(body)

    def layer(l, _):
        pl.when(l == 0)(shorts_arrive)
        if fast:
            gather_got(wall.at[l], l, 2)
        conv_pass(l, LONG)
        matmul_pass(l, LONG)
        conv_pass(l, SHORT)
        matmul_pass(l, SHORT)
        send_stats(l)

        def halo_out():
            put_edges(lambda row: pre[l, row : row + 1, :], l)
            edges(hsend.at[l], hh.at[l, 0:8], hh.at[l, 8:16], sem_hs.at[l], sem_hr.at[l], True)

        sync_core(l, halo_out)
        sync_send(l)

        if fast:
            gather_got(wall.at[l + 1], l + 1, 1)
            gather_stage(wall.at[l + 1], l + 1, 2)

        pl.when(l > 0)(lambda: prep_pass(l - 1))

        @pl.when(l == 0)
        def _():
            load_g.wait()
            stage_short()
            to_perm_long(xv[long_at], cot, lambda u: u * UR)

        @pl.when(l == 1)
        def _():
            one_hot(back_l, F, True)
            one_hot(back_s, UR, True)

        @pl.when(l == LAYERS - 1)
        def _():
            for k in range(U - 1):
                cot_piece(k, 1)

            @pl.when(tm > 0)
            def _():
                for k in range(U - 1):
                    total_wait(gin4.at[k], sem_cr.at[S2 + k])

            to_perm_short(gin4, cot, lambda u: u * UR, True)

        if fast:
            @pl.when(l + 2 < MATS)
            def _():
                gather_got(wall.at[l + 2], l + 2, 0)
                gather_stage(wall.at[l + 2], l + 2, 1)

            @pl.when(l + 3 < MATS)
            def _():
                gather_stage(wall.at[l + 3], l + 3, 0)

        total = sync_done(l)
        edges(hsend.at[l], hh.at[l, 0:8], hh.at[l, 8:16], sem_hs.at[l], sem_hr.at[l], False)
        for k in range(U - 1):
            pl.when(l == k)(functools.partial(cot_piece, k, 0))
        scale = wide(inv_count)
        mean = total[0:1] * scale
        var = total[1:2] * scale - mean * mean
        inv = lax.rsqrt(var + NORM_EPSILON)
        ga = small[pl.ds(AT_GAMMA + l, 1), :]
        a = ga * inv
        coef[l, 0:1, :] = 0.5 * a
        coef[l, 1:2, :] = 0.5 * (small[pl.ds(AT_BETA + l, 1), :] - mean * a)
        coef[l, 2:3, :] = mean
        coef[l, 3:4, :] = inv
        coef[l, 4:5, :] = a

        pl.when(l < LAYERS - 1)(lambda: act_pass(l))
        return 0

    lax.fori_loop(0, LAYERS, layer, 0)

    top = LAYERS - 1
    pool[...] = jnp.zeros(pool.shape, F32)

    def last_act(j, _):
        a, b = coef[top, 0:1, lane(j)], coef[top, 1:2, lane(j)]
        acc = None
        for u in range(NU):
            v = pre[top, u * UR : (u + 1) * UR, lane(j)] * a + b
            v = v + v * jnp.tanh(v)
            if u >= 4:
                v = v * mask[(u - 4) * UR : (u - 3) * UR, :]
            act[u * UR : (u + 1) * UR, lane(j)] = v
            f = fold8(v)
            acc = f if u == 0 or u >= 4 else acc + f
            if u >= 3:
                pool[u - 3 : u - 2, lane(j)] = jnp.sum(acc, axis=0, keepdims=True)
        return 0

    each_lane(last_act)

    def time_sum(s, value):
        tsend[s] = value
        ds = [remote(tsend.at[s], trecv.at[s, i - 1], sem_ts.at[s], sem_tr.at[s], (dp, lax.rem(tm + i, TM))) for i in range(1, TM)]
        for d in ds:
            d.start()

    def time_done(s):
        whole = trecv.at[s]
        total_wait(whole, sem_tr.at[s])
        total_wait(whole, sem_ts.at[s])
        total = tsend[s]
        for i in range(TM - 1):
            total = total + trecv[s, i]
        return total

    e8 = lax.broadcasted_iota(jnp.int32, (8, LANES), 0)
    len8 = jnp.full((8, LANES), F * TM, jnp.int32)
    for k in range(U - 1):
        len8 = jnp.where(e8 == k + 1, short_len[k], len8)
    inv_len = 1.0 / len8.astype(F32)
    live = jnp.where(e8 < U, 1.0, 0.0)
    time_sum(0, pool[...])
    prep_pass(top)
    if fast:
        gather_got(wall.at[LAYERS], LAYERS, 2)
    resd[0:F, :] = dot(ypad[0, 32 : 32 + F, :], weights(LAYERS))
    for u in SHORT:
        resd[u * UR : (u + 1) * UR, :] = dot(ypad[0, win(u) + 32 : win(u) + 32 + UR, :], weights(LAYERS))
    p = time_done(0) * wide(inv_len)
    sq = squeeze_all()
    ex = small[0:SE, :].astype(BF16)
    q = dot_parts(p, sq)
    sig_q = logistic(q)
    z_act = q * sig_q
    gate[...] = logistic(dot_parts(z_act, ex))
    pool[...] = jnp.zeros(pool.shape, F32)

    def top_pass(j, _):
        acc = None
        for u in range(NU):
            rs = slice(u * UR, (u + 1) * UR)
            seg = seg_of(u)
            av = act[rs, lane(j)]
            half = 0.5 * (av * gate[seg : seg + 1, lane(j)] + resd[rs, lane(j)])
            t = jnp.tanh(half)
            out = half + half * t
            slope = (0.5 + 0.5 * t) * (1.0 + half * (1.0 - t))
            dv = cot[rs, lane(j)].astype(F32) * slope
            if u >= 4:
                out = out * mask[(u - 4) * UR : (u - 3) * UR, :]
            outp[rs, lane(j)] = out.astype(BF16)
            du[rs, lane(j)] = dv
            drl[rs, lane(j)] = dv.astype(BF16)
            f = fold8(dv * av)
            acc = f if u == 0 or u >= 4 else acc + f
            if u >= 3:
                pool[u - 3 : u - 2, lane(j)] = jnp.sum(acc, axis=0, keepdims=True)
        return 0

    each_lane(top_pass)
    time_sum(1, pool[...])

    def back_long(buf, src):
        for u in range(4):
            buf[0, u * UR : (u + 1) * UR, :] = dot(back_l[u * UR : (u + 1) * UR, :], src[0:F, :]).astype(BF16)

    def back_short(buf, stage, src):
        for k in range(U - 1):
            stage[k] = dot(back_s[...], src[F + k * UR : F + (k + 1) * UR, :]).astype(BF16)

        @pl.when(tm >= N_SRC)
        def _():
            for k in range(U - 1):
                buf[1 + k] = jnp.zeros((F, C), BF16)

        @pl.when(first)
        def _():
            for k in range(U - 1):
                buf[1 + k, 0:UR, :] = stage[k]

    def back_piece(buf, stage, sems, rsems, k):
        owner, q = tm // 4, lax.rem(tm, 4)
        dst = buf.at[1 + k, pl.ds(pl.multiple_of(q * UR, UR), UR), :]
        return remote(stage.at[k], dst, sems.at[k], rsems.at[k, q], (dp, owner))

    def back_send(buf, stage, sems, rsems, ks):
        @pl.when(tm > 0)
        def _():
            for k in ks:
                back_piece(buf, stage, sems, rsems, k).start()

    def back_left(buf, stage, sems, rsems):
        @pl.when(tm > 0)
        def _():
            for k in range(U - 1):
                back_piece(buf, stage, sems, rsems, k).wait_send()

    def back_arrived(buf, rsems, k):
        @pl.when(tm < N_SRC)
        def _():
            for i in range(4):
                got = functools.partial(total_wait, buf.at[1 + k, i * UR : (i + 1) * UR, :], rsems.at[k, i])
                if i == 0:
                    pl.when(tm > 0)(got)
                else:
                    got()

    def back_done(buf, stage, sems, rsems):
        back_left(buf, stage, sems, rsems)
        for k in range(U - 1):
            back_arrived(buf, rsems, k)

    put_out = pltpu.make_async_copy(obuf, out_any, sem_loc.at[2])
    back_long(obuf, outp)
    back_short(obuf, xin, outp)

    def xrows(u):
        o = win(u) + 32
        return ypad[0, o : o + UR, :]

    def put_grad(m, total):
        if fast:
            big.send[m] = total.astype(BF16).reshape(Z, 2, Y, 2, SH, C)
            big.go(m, 0)
        else:
            gp[...] = total
            pltpu.make_async_copy(gp, env["gmats"].at[m], sem_loc.at[1]).start()

    def grad_gone():
        if not fast:
            pltpu.make_async_copy(gp, env["gmats"].at[0], sem_loc.at[1]).wait()

    def xrows(u):
        o = win(u) + 32
        return ypad[0, o : o + UR, :]

    def resid_grads():
        total = dot(ypad[0, 32 : 32 + F, :], drl[0:F, :], ((0,), (0,)))
        for u in SHORT:
            total = total + dot(xrows(u), drl[u * UR : (u + 1) * UR, :], ((0,), (0,)))
        put_grad(LAYERS, total)
        gres_in[...] = dot(drl[...], weights(LAYERS), ((1,), (1,)))

    resid_grads()
    dg = time_done(1)
    gv = gate[...]
    de = dg * gv * (1.0 - gv) * wide(live)
    dz = dot_parts(de, ex, ((1,), (1,)))
    dq = dz * sig_q * (1.0 + q * (1.0 - sig_q))
    cvec[...] = dot_parts(dq, sq, ((1,), (1,))) * wide(inv_len)
    fac[0], fac[1] = p, de
    facs[0], facs[1] = z_act, dq

    def pair_grads():
        lead = jnp.where(first, 1.0, 0.0)
        zero = jnp.zeros((C, LANES - 2 * SE), F32)
        pair = [dot(fac[1 - i], facs[i], ((0,), (0,)), precision=HIGHEST) for i in range(2)]
        pair = jnp.concatenate(pair + [zero] * (LANES > 2 * SE), axis=1) * lead
        if fast:
            little.send[0] = pair.reshape(Z, 2, Y, 2, SH, LANES)
            little.go(0, 0)
        else:
            env["gpair"][...] = pair

    def back_sums(l, s, grad_of):
        def body(j, _):
            acc0 = acc1 = None
            make = grad_of(j)
            for u in range(NU):
                rs = slice(u * UR, (u + 1) * UR)
                v = make(u) * slope[l, rs, lane(j)].astype(F32)
                xc = pre[l, rs, lane(j)]
                dn[u * UR : (u + 1) * UR, lane(j)] = v
                f0, f1 = fold8(v), fold8(v * xc)
                acc0 = f0 if u == 0 else acc0 + f0
                acc1 = f1 if u == 0 else acc1 + f1
            send_a[s, 0:1, lane(j)] = jnp.sum(acc0, axis=0, keepdims=True)
            send_a[s, 1:2, lane(j)] = jnp.sum(acc1, axis=0, keepdims=True)
            return 0

        each_lane(body)

    def top_grad(j):
        def make(u):
            seg = seg_of(u)
            return du[u * UR : (u + 1) * UR, lane(j)] * gate[seg : seg + 1, lane(j)] + cvec[seg : seg + 1, lane(j)]
        return make

    def conv_grad(l):
        def outer(j):
            w = tap_rows(l, j)

            def make(u):
                o = win(u)
                v = ddpad[o : o + UR + 64, lane(j)].astype(F32)
                t = v[64 : 64 + UR] * w[0]
                for k in range(1, KERNEL):
                    t = t + v[64 - 16 * k : 64 - 16 * k + UR] * w[k]
                return t
            return make
        return outer

    back_sums(top, LAYERS, top_grad)

    def point_grad(l):
        grad_gone()
        put_grad(l, dot(dlow[l], dhl[0:R, :], ((0,), (0,))))

    def depth_grad(l):
        def body(j, _):
            acc = [None] * KERNEL
            for u in range(NU):
                o = win(u)
                v = ypad[l, o : o + UR + 64, lane(j)].astype(F32)
                g = ddpad[o + 32 : o + 32 + UR, lane(j)].astype(F32)
                for k in range(KERNEL):
                    f = fold8(v[16 * k : 16 * k + UR] * g)
                    acc[k] = f if u == 0 else acc[k] + f
            rows = [jnp.sum(acc[k], axis=0, keepdims=True) for k in range(KERNEL)]
            rows.append(jnp.zeros((8 - KERNEL, LANES), F32))
            at = pl.ds(pl.multiple_of(AT_TAPS + 8 * l, 8), 8)
            gsmall[at, lane(j)] = jnp.concatenate(rows, axis=0)
            return 0

        each_lane(body)
    def dh_pass(l, units):
        def body(j, _):
            a, k1, k0 = (coef[l, r : r + 1, lane(j)] for r in (4, 5, 6))
            for u in units:
                rs = slice(u * UR, (u + 1) * UR)
                v = dn[rs, lane(j)] * a - (pre[l, rs, lane(j)] * k1 + k0)
                if u >= 4:
                    v = v * mask[(u - 4) * UR : (u - 3) * UR, :]
                dhl[rs, lane(j)] = v.astype(BF16)
            if units is SHORT:
                v = (dhh[l, :, lane(j)] * a - (hx[l, :, lane(j)] * k1 + k0)) * hmask[...]
                dhl[R : R + 16, lane(j)] = v.astype(BF16)
            return 0

        each_lane(body)

    def dd_pass(l):
        dh_pass(l, LONG)
        ddpad[32 : 32 + F, :] = dot(dhl[0:F, :], weights(l), ((1,), (1,))).astype(BF16)
        dh_pass(l, SHORT)
        v = dot(dhl[F : R + 16, :], weights(l), ((1,), (1,)))
        for u in SHORT:
            ddpad[win(u) + 32 : win(u) + 32 + UR, :] = v[(u - 4) * UR : (u - 3) * UR].astype(BF16)
        hx[l] = v[R - F : R - F + 16].astype(BF16).astype(F32)

        def pad(j, _):
            pads_from(ddpad, j, hx[l, :, lane(j)], range(U))
            return 0

        each_lane(pad)

    def back_layer(step, _):
        l = top - step
        s = LAYERS + step

        def halo_out():
            put_edges(lambda row: dn[row : row + 1, :], s)
            edges(hsend.at[s], dhh.at[l, 0:8], dhh.at[l, 8:16], sem_hs.at[s], sem_hr.at[s], True)

        sync_core(s, halo_out)
        sync_send(s)

        @pl.when(step > 0)
        def _():
            point_grad(l + 1)
            depth_grad(l + 1)

        pl.when(step == 0)(pair_grads)

        @pl.when(step == LAYERS - 1)
        def _():
            back_done(obuf, xin, sem_os.at[0], sem_or.at[0])
            put_out.start()

        if fast:
            @pl.when(step == 1)
            def _():
                little.core_to_x(0)

            @pl.when(step == 2)
            def _():
                little.x_to_plane(0)

            @pl.when(step > 0)
            def _():
                big.x_sum(l + 2)

            @pl.when(step > 1)
            def _():
                env["keep"][l + 3] = big.result(l + 3)

            big.core_to_x(l + 1)

        if fast:
            pl.when(step > 0)(lambda: big.go(l + 2, 2))

        total = sync_done(s)
        @pl.when(step < U - 1)
        def _():
            back_send(obuf, xin, sem_os.at[0], sem_or.at[0], [step])

        edges(hsend.at[s], dhh.at[l, 0:8], dhh.at[l, 8:16], sem_hs.at[s], sem_hr.at[s], False)
        ggb[l, 0:2, :] = total
        a = coef[l, 4:5, :]
        coef[l, 5:6, :] = a * total[1:2] * wide(inv_count)
        coef[l, 6:7, :] = a * total[0:1] * wide(inv_count)

        dd_pass(l)

        @pl.when(l > 0)
        def _():
            back_sums(l - 1, s + 1, conv_grad(l - 1))
        return 0

    def run_back():
        lax.fori_loop(0, LAYERS, back_layer, 0)

    conv_grad_of = conv_grad

    def conv_grad(l):
        return conv_grad_of(l + 1)

    gsmall[...] = jnp.zeros(gsmall.shape, F32)
    run_back()
    lead_all = jnp.where(first & (dp == 0), 1.0, 0.0)
    for l in range(LAYERS):
        gsmall[AT_BETA + l : AT_BETA + l + 1, :] = ggb[l, 0:1, :] * lead_all
        gsmall[AT_GAMMA + l : AT_GAMMA + l + 1, :] = ggb[l, 1:2, :] * lead_all
    def final_pass(units):
        def body(j, _):
            make = conv_grad_of(0)(j)
            for u in units:
                rs = slice(u * UR, (u + 1) * UR)
                v = make(u)
                if u >= 4:
                    v = v * mask[(u - 4) * UR : (u - 3) * UR, :]
                outp[rs, lane(j)] = (v + gres_in[rs, lane(j)]).astype(BF16)
            return 0

        each_lane(body)

    final_pass(SHORT)
    back_short(gbuf, gin4, outp)
    back_send(gbuf, gin4, sem_os.at[1], sem_or.at[1], range(U - 1))
    point_grad(0)
    if fast:
        big.core_to_x(0)
    depth_grad(0)
    if fast:
        for j in range(NL):
            rows = gsmall[:, j * LANES : (j + 1) * LANES].T
            part = rows.reshape(LANES // (2 * SH), 2, SH, LANES)
            per = LANES // (2 * SH)
            for i in range(per):
                n = j * per + i
                little.send[1, n // (2 * Y), n // Y % 2, n % Y] = part[i]
        little.go(1, 0)
        big.x_to_plane(1)
    final_pass(LONG)
    back_long(gbuf, outp)
    put_gin = [pltpu.make_async_copy(gbuf.at[k], gin_any.at[k], sem_loc.at[3 + k]) for k in range(U)]
    put_gin[0].start()
    if fast:
        little.core_to_x(1)
        env["keep"][2] = big.result(2)
        big.x_to_plane(0)
        little.x_to_plane(1)
        env["keep_s"][0] = little.result(0)
        env["keep"][1] = big.result(1)
        early = pltpu.make_async_copy(env["keep"].at[1:MATS], env["gmats"].at[1:MATS], env["sem_keep"].at[0])
        early.start()
        for m in range(1, MATS):
            big.left(m)
            gather_left(wall.at[m], m)
        for buf, m in halves:
            gather_left(buf, m)
        little.left(0)
        gather_left(sall, MATS)
    else:
        env["grows"][...] = gsmall[...]
    for k in range(U - 1):
        back_arrived(gbuf, sem_or.at[1], k)
        put_gin[1 + k].start()
    back_left(gbuf, gin4, sem_os.at[1], sem_or.at[1])
    if fast:
        env["keep"][0] = big.result(0)
        late = [pltpu.make_async_copy(env["keep"].at[0], env["gmats"].at[0], env["sem_keep"].at[1])]
        late[0].start()
        env["keep_s"][1] = little.result(1)
        late.append(pltpu.make_async_copy(env["keep_s"].at[0], env["gpair"], env["sem_keep"].at[2]))
        late.append(pltpu.make_async_copy(env["keep_s"].at[1], env["grows"], env["sem_keep"].at[3]))
        late[1].start()
        late[2].start()
        big.left(0)
        little.left(1)
    grad_gone()
    put_out.wait()
    for c in put_gin:
        c.wait()
    if fast:
        for c in [early] + late:
            c.wait()


def finish_kernel(cfg, lengths, out_s, gin_s, gmats_any, gpair_any, grows_any, *rest):
    DP, TM, U, F, C, SE, SH, LAYERS, KERNEL, fast = cfg
    out, gin, gdepth_any, gpoint, ggamma_any, gbeta_any, gsq_any, gex_any, gres = rest[:9]
    hold, gmats, gpair, grows, turn, gdepth, ggamma, gbeta, gsq, gex, sems, sems_g = rest[9:]
    dp = lax.axis_index("dp")
    long_at = jnp.int32(0)
    for b in range(1, U):
        long_at = jnp.where(lengths[dp * U + b] == F * TM, jnp.int32(b), long_at)
    copies = []
    loads = [
        pltpu.make_async_copy(src, dst, sems_g.at[i])
        for i, (src, dst) in enumerate(((gmats_any, gmats), (gpair_any, gpair), (grows_any, grows)))
    ]
    for c in loads:
        c.start()
    for b in range(U):
        slot = jnp.where(b == long_at, 0, jnp.where(b < long_at, b + 1, b))
        for i, (src, dst) in enumerate(((out_s, out), (gin_s, gin))):
            get = pltpu.make_async_copy(src.at[slot], hold.at[i, b], sems.at[0, i, b])
            put = pltpu.make_async_copy(hold.at[i, b], dst.at[b], sems.at[1, i, b])
            copies.append((get, put))
            get.start()
    loads[0].wait()
    results = [
        pltpu.make_async_copy(gmats.at[0:LAYERS], gpoint, sems_g.at[3]),
        pltpu.make_async_copy(gmats.at[LAYERS], gres, sems_g.at[4]),
    ]
    for c in results:
        c.start()
    for get, put in copies:
        get.wait()
        put.start()
    for c in loads[1:]:
        c.wait()
    at_taps = SE
    at_gamma = SE + 8 * LAYERS
    at_beta = at_gamma + 8
    gsq[...] = gpair[:, SE : 2 * SE]
    gex[...] = gpair[:, 0:SE]
    turn[...] = jnp.zeros(turn.shape, F32)
    turn[0:SH] = grows[...]
    turn[...] = turn[...].T
    for l in range(LAYERS):
        gdepth[l] = turn[at_taps + 8 * l : at_taps + 8 * l + KERNEL, 0:SH]
    ggamma[...] = turn[at_gamma : at_gamma + LAYERS, 0:SH]
    gbeta[...] = turn[at_beta : at_beta + LAYERS, 0:SH]
    pairs = ((gdepth, gdepth_any), (ggamma, ggamma_any), (gbeta, gbeta_any), (gsq, gsq_any), (gex, gex_any))
    for i, (src, dst) in enumerate(pairs):
        results.append(pltpu.make_async_copy(src, dst, sems_g.at[5 + i]))
        results[-1].start()
    for _, put in copies:
        put.wait()
    for c in results:
        c.wait()


def local(sizes, inputs, lengths, depth_w, point_w, gamma, beta, squeeze_w, excite_w, resid_w, cotangent):
    DP, TM = sizes
    U, F, C = inputs.shape
    LAYERS, KERNEL, SH = depth_w.shape
    SE = squeeze_w.shape[1]
    UR = F // 4
    NU = 4 + U - 1
    R = NU * UR
    RP = F + 64 + (U - 1) * (UR + 64)
    S = 2 * LAYERS
    chips = DP * (TM // 2) - 1
    axes = ("dp", "tm")
    fast = SH % 16 == 0 and DP % 2 == 0 and DP > 2
    Z, Y = DP // 2, TM // 2
    MATS = LAYERS + 1
    vm = pltpu.VMEM
    dma = pltpu.SemaphoreType.DMA
    any_spec = pl.BlockSpec(memory_space=pl.ANY)
    vm_spec = pl.BlockSpec(memory_space=pltpu.VMEM)
    sm_spec = pl.BlockSpec(memory_space=pltpu.SMEM)
    sd = jax.ShapeDtypeStruct
    cfg = (DP, TM, U, F, C, SE, SH, LAYERS, KERNEL, fast)
    at_gamma = SE + 8 * LAYERS
    operands = dict(lengths=lengths, x_any=inputs, g_any=cotangent)
    specs = [sm_spec, any_spec, any_spec]
    outs = dict(out_any=sd((U, F, C), BF16), gin_any=sd((U, F, C), BF16))
    out_specs = [any_spec, any_spec]
    if fast:
        operands.update(
            point=point_w, taps=depth_w, gamma=gamma, beta=beta, squeeze=squeeze_w, excite=excite_w.T, resid=resid_w
        )
        specs += [vm_spec] * 7
        outs.update(gmats=sd((MATS, SH, C), F32), gpair=sd((SH, LANES), F32), grows=sd((SH, LANES), F32))
        out_specs += [any_spec] * 3
    else:
        mats = jnp.concatenate([point_w, resid_w[None]], axis=0)
        depth_rows = jnp.pad(depth_w, ((0, 0), (0, 8 - KERNEL), (0, 0))).reshape(8 * LAYERS, SH)
        fill = ((0, 8 - LAYERS), (0, 0))
        rows = jnp.concatenate([excite_w, depth_rows, jnp.pad(gamma, fill), jnp.pad(beta, fill)], axis=0)
        rows = jnp.pad(rows, ((0, LANES - rows.shape[0]), (0, 0)))
        operands.update(
            mats=lax.all_gather(mats, axes, axis=1, tiled=True),
            small_in=lax.all_gather(rows, axes, axis=1, tiled=True).astype(F32),
            squeeze=lax.all_gather(squeeze_w, axes, axis=0, tiled=True),
        )
        specs += [vm_spec] * 3
        outs.update(gmats=sd((MATS, C, C), F32), gpair=sd((C, LANES), F32), grows=sd((LANES, C), F32))
        out_specs += [any_spec, vm_spec, vm_spec]
    scratch = dict(
        xv=vm((U, F, C), BF16), xs=vm((U - 1, F, C), BF16), edge=vm((2, 16, C), BF16),
        xin=vm((U - 1, UR, C), BF16), gin4=vm((U - 1, UR, C), BF16),
        halo_l=vm((4, 16, C), BF16), halo_r=vm((4, 16, C), BF16),
        cot=vm((R, C), BF16), ypad=vm((LAYERS, RP, C), BF16), dlow=vm((LAYERS, R, C), BF16),
        pre=vm((LAYERS, R, C), F32), hh=vm((LAYERS, 16, C), F32), hx=vm((LAYERS, 16, C), F32),
        mask=vm(((U - 1) * UR, LANES), F32), hmask=vm((16, LANES), F32), coef=vm((LAYERS, 8, C), F32),
        resd=vm((R, C), F32), act=vm((R, C), F32), du=vm((R, C), F32), drl=vm((R, C), BF16),
        dhl=vm((R + 16, C), BF16), ddpad=vm((RP, C), BF16),
        perm_l=vm((F, F), BF16), perm_s=vm((UR, UR), BF16), back_l=vm((F, F), BF16), back_s=vm((UR, UR), BF16),
        outp=vm((R, C), BF16), obuf=vm((U, F, C), BF16), gbuf=vm((U, F, C), BF16),
        small=vm((LANES, C), F32), slope=vm((LAYERS, R, C), BF16),
        fac=vm((2, 8, C), F32), facs=vm((2, 8, SE), F32), gsmall=vm((LANES, C), F32), ggb=vm((LAYERS, 8, C), F32),
        sums=vm((2, 8, C), F32), send_a=vm((S, 2, C), F32), send_b=vm((S, 2, C), F32),
        recv_core=vm((S, 2, C), F32), recv_chip=vm((S, chips + 1, 2, C), F32),
        hsend=vm((S, 2, 8, C), F32), dhh=vm((LAYERS, 16, C), F32),
        tsend=vm((2, 8, C), F32), trecv=vm((2, TM - 1, 8, C), F32),
        pool=vm((8, C), F32), gate=vm((8, C), F32), cvec=vm((8, C), F32),
        sem_loc=dma((3 + U,)), sem_cs=dma((S,)), sem_cr=dma((S + U - 1,)), sem_cot=dma((U - 1, 4)), sem_ks=dma((S,)), sem_kr=dma((S,)),
        sem_hs=dma((S, 2)), sem_hr=dma((S, 2)), sem_ts=dma((2,)), sem_tr=dma((2,)),
        sem_xs=dma((14,)), sem_xr=dma((5,)), sem_os=dma((2, U - 1)), sem_or=dma((2, U - 1, 4)),
    )
    if fast:
        scratch.update(
            wall=vm((MATS, Z, 2, Y, 2, SH, C), BF16), sall=vm((Z, 2, Y, 2, SH, 2 * LANES), BF16),
            pack=vm((LANES, LANES), F32), keep=vm((MATS, SH, C), F32), keep_s=vm((2, SH, LANES), F32),
            sem_keep=dma((4,)), sem_gs=dma((MATS + 1, 3)), sem_gr=dma((MATS + 1, 3)),
        )
        for name, n, cols, kind in (("big", MATS, C, BF16), ("little", 2, LANES, F32)):
            scratch.update(
                {
                    name + "_send": vm((n, Z, 2, Y, 2, SH, cols), kind),
                    name + "_core": vm((n, Z, 2, Y, SH, cols), kind),
                    name + "_xsum": vm((n, 2, Z, Y, SH, cols), kind),
                    name + "_rx": vm((n, Z, Y, SH, cols), kind),
                    name + "_zsum": vm((n, Z, Y, SH, cols), kind),
                    name + "_rz": vm((n, Z * Y - 1, SH, cols), kind),
                    name + "_ss": dma((n, 3)),
                    name + "_rs": dma((n, 3)),
                }
            )
    if not fast:
        scratch.update(gp=vm((C, C), F32))
    names = list(operands) + list(outs) + list(scratch)
    out_s, gin_s, gmats, gpair, grows = pl.pallas_call(
        functools.partial(block_kernel, cfg, names),
        out_shape=tuple(outs.values()),
        in_specs=specs,
        out_specs=tuple(out_specs),
        scratch_shapes=list(scratch.values()),
        compiler_params=pltpu.CompilerParams(collective_id=0, has_side_effects=True, vmem_limit_bytes=63 << 20),
    )(*operands.values())
    if not fast:
        gmats = lax.psum_scatter(gmats, axes, scatter_dimension=1, tiled=True)
        gpair = lax.psum_scatter(gpair, axes, scatter_dimension=0, tiled=True)
        grows = lax.psum_scatter(grows, axes, scatter_dimension=1, tiled=True).T
    sizes_out = (
        ((U, F, C), BF16), ((U, F, C), BF16), ((LAYERS, KERNEL, SH), F32), ((LAYERS, SH, C), F32), ((LAYERS, SH), F32),
        ((LAYERS, SH), F32), ((SH, SE), F32), ((SH, SE), F32), ((SH, C), F32),
    )
    done = pl.pallas_call(
        functools.partial(finish_kernel, cfg),
        out_shape=tuple(sd(*size) for size in sizes_out),
        in_specs=[sm_spec] + [any_spec] * 5,
        out_specs=(any_spec,) * 9,
        scratch_shapes=[
            vm((2, U, F, C), BF16), vm((MATS, SH, C), F32), vm((SH, LANES), F32), vm((SH, LANES), F32),
            vm((LANES, LANES), F32),
            vm((LAYERS, KERNEL, SH), F32), vm((LAYERS, SH), F32), vm((LAYERS, SH), F32), vm((SH, SE), F32),
            vm((SH, SE), F32), dma((2, 2, U)), dma((10,)),
        ],
    )(lengths, out_s, gin_s, gmats, gpair, grows)
    return done[:7] + (done[7].T, done[8])


def solution(mesh):
    both = ("dp", "tm")
    rows, cols = P(both, None), P(None, both)
    frames = P("dp", "tm", None)
    taps, mats = P(None, None, both), P(None, both, None)
    sizes = (mesh.shape["dp"], mesh.shape["tm"])
    return jax.shard_map(
        functools.partial(local, sizes),
        mesh=mesh,
        in_specs=(frames, P(), taps, mats, cols, cols, rows, cols, rows, frames),
        out_specs=(frames, frames, taps, mats, cols, cols, rows, cols, rows),
        check_vma=False,
    )
```

profile of v0, /device:TPU:0, one launch (start us, length us, event | category | flops | bytes accessed | tf_op | source)
XLA Modules:
  0.0 124.9 jit_solution(15305853821722106487)
XLA Ops:
  0.6 119.4 %shard_map.169 = (bf16[4,512,512]{2,1,0:T(8,128)(2,1)}, bf16[4,512,512]{2,1,0:T(8,128)(2,1)}, f32[6,16,512]{2,1,0:T(8,128)}, f32[16,128]{1,0:T(8,128)}, f32[16,128]{1,0:T(8,128)}) custom-call(s32[32]{0:T(128)} %lengths.1, bf16[4,512,512]{2,1,0:T(8,128)(2,1)} %refs_1_.1, bf16[4,512,512]{2,1,0:T(8,128)(2,1)} %refs_2_.1, bf16[5,16,512]{2,1,0:T(8,128)(2,1)} %refs_3_.1, ...), custom_call_target="tpu_custom_call" | custom-call | tf_op jit(solution)/shard_map/pallas_call | solution.py:1271
  120.0 4.7 %shard_map.170 = (bf16[4,512,512]{2,1,0:T(8,128)(2,1)}, bf16[4,512,512]{2,1,0:T(8,128)(2,1)}, f32[5,5,16]{2,1,0:T(8,128)}, f32[5,16,512]{2,1,0:T(8,128)}, f32[5,...) custom-call(s32[32]{0:T(128)} %lengths.1, ...), custom_call_target="tpu_custom_call" | custom-call | tf_op jit(solution)/shard_map/pallas_call | solution.py:1287
where the time goes:
time: 125 us
  Pallas kernels  124 us (99%)
    pallas_call x1, Pallas kernels, local(): pl.pallas_call(functools.partial(block_kernel, cfg, names), out_shape=tup...  119 us
    pallas_call x1, Pallas kernels, local(): pl.pallas_call(functools.partial(finish_kernel, cfg), out_shape=tuple((sd...  4.7 us

commit v1 on v0

--- a/solution.py
+++ b/solution.py
@@ -337,9 +337,12 @@
         sall[z, x, y, core, :, 0:LANES] = pack[0:SH, :].astype(BF16)
         pack[0:SH, 0:SE] = env["squeeze"][...].astype(F32)
         sall[z, x, y, core, :, LANES : 2 * LANES] = pack[0:SH, :].astype(BF16)
-        for l in range(LAYERS):
-            wall[l, z, x, y, core] = env["point"][l]
-        wall[LAYERS, z, x, y, core] = env["resid"][...]
+        shares = [env["point"].at[l] for l in range(LAYERS)] + [env["resid"]]
+        loads = [
+            pltpu.make_async_copy(src, wall.at[m, z, x, y, core], env["sem_in"].at[m]) for m, src in enumerate(shares)
+        ]
+        for c in loads:
+            c.start()
     else:
         def weights(m):
             return env["mats"][m]
@@ -427,6 +430,9 @@
 
     y0 = ypad.at[0]
     zero_ends()
+    if fast:
+        for c in loads:
+            c.wait()
     pl.semaphore_wait(barrier, len(chips) + len(others))
     if fast:
         gather_stage(sall, MATS, 0)
@@ -1207,7 +1213,7 @@
         operands.update(
             point=point_w, taps=depth_w, gamma=gamma, beta=beta, squeeze=squeeze_w, excite=excite_w.T, resid=resid_w
         )
-        specs += [vm_spec] * 7
+        specs += [any_spec] + [vm_spec] * 5 + [any_spec]
         outs.update(gmats=sd((MATS, SH, C), F32), gpair=sd((SH, LANES), F32), grows=sd((SH, LANES), F32))
         out_specs += [any_spec] * 3
     else:
@@ -1250,7 +1256,7 @@
         scratch.update(
             wall=vm((MATS, Z, 2, Y, 2, SH, C), BF16), sall=vm((Z, 2, Y, 2, SH, 2 * LANES), BF16),
             pack=vm((LANES, LANES), F32), keep=vm((MATS, SH, C), F32), keep_s=vm((2, SH, LANES), F32),
-            sem_keep=dma((4,)), sem_gs=dma((MATS + 1, 3)), sem_gr=dma((MATS + 1, 3)),
+            sem_keep=dma((4,)), sem_in=dma((MATS,)), sem_gs=dma((MATS + 1, 3)), sem_gr=dma((MATS + 1, 3)),
         )
         for name, n, cols, kind in (("big", MATS, C, BF16), ("little", 2, LANES, F32)):
             scratch.update(

time: 125 us -> 125 us (level)
  no operation moved by 1% of the time
where the time goes in v1:
time: 125 us
  Pallas kernels  124 us (99%)
    pallas_call x1, Pallas kernels, local(): pl.pallas_call(functools.partial(block_kernel, cfg, names), out_shape=tup...  119 us
    pallas_call x1, Pallas kernels, local(): pl.pallas_call(functools.partial(finish_kernel, cfg), out_shape=tuple((sd...  4.7 us

profile of v1, /device:TPU:0, one launch (start us, length us, event | category | flops | bytes accessed | tf_op | source)
XLA Modules:
  0.0 124.8 jit_solution(2996503726598476398)
XLA Ops:
  0.6 119.3 %shard_map.169 = (bf16[4,512,512]{2,1,0:T(8,128)(2,1)}, bf16[4,512,512]{2,1,0:T(8,128)(2,1)}, f32[6,16,512]{2,1,0:T(8,128)}, f32[16,128]{1,0:T(8,128)}, f32[16,128]{1,0:T(8,128)}) custom-call(s32[32]{0:T(128)} %lengths.1, bf16[4,512,512]{2,1,0:T(8,128)(2,1)} %refs_1_.1, bf16[4,512,512]{2,1,0:T(8,128)(2,1)} %refs_2_.1, bf16[5,16,512]{2,1,0:T(8,128)(2,1)} %refs_3_.1, ...), custom_call_target="tpu_custom_call" | custom-call | tf_op jit(solution)/shard_map/pallas_call | solution.py:1277
  120.0 4.7 %shard_map.170 = (bf16[4,512,512]{2,1,0:T(8,128)(2,1)}, bf16[4,512,512]{2,1,0:T(8,128)(2,1)}, f32[5,5,16]{2,1,0:T(8,128)}, f32[5,16,512]{2,1,0:T(8,128)}, f32[5,...) custom-call(s32[32]{0:T(128)} %lengths.1, ...), custom_call_target="tpu_custom_call" | custom-call | tf_op jit(solution)/shard_map/pallas_call | solution.py:1293
